TPU v7x, 256 devices: a whole 4x4x8 slice. The times are simulated.
256 devices in a mesh: dp: 32 (over z_lo, y, core), feat: 8 (over z_hi, x).
Axes of the slice: x: 4, y: 4, z: 8 (z_hi: 2, z_lo: 4; z = z_hi * 4 + z_lo), core: 2. Of those that a mesh axis runs over, the one named last changes fastest.
Arguments:
- table: bfloat16 [4096, 3584], P('dp', 'feat'), may hold values from -64 to 64
- text: bfloat16 [4096, 3584], P('dp', 'feat'), may hold values from -64 to 64
- table_proj: bfloat16 [3584, 4096], P(None, 'feat'), may hold values from -1 to 1
- text_proj: bfloat16 [3584, 4096], P(None, 'feat'), may hold values from -1 to 1
Outputs:
- grad_table: float32 [4096, 3584], P('dp', 'feat')
- grad_text: float32 [4096, 3584], P('dp', 'feat')
- loss_mean: float32 [1], replicated
All inputs are finite; a program needn't handle non-finite values.
Results may differ from a plain program's by a relative error of at most 0.0044.
Values may be sent and summed in bfloat16 or wider, within the bound.
A program may use at most 64 MiB of HBM per device.

v0:
```python
import jax
import jax.numpy as jnp
from jax import lax
from jax.sharding import PartitionSpec as P

OFF_WEIGHT = 0.1
EPS = 1e-05


def normalize(proj, total, squares, pairs):
    center = total / pairs
    spread = squares / pairs - center * center
    inverse = lax.rsqrt(spread + EPS)
    return ((proj - center) * inverse, inverse)


def kernel_block(corr_block, row_index, col_index):
    on_diag = row_index[:, None] == col_index[None, :]
    terms = jnp.where(
        on_diag, (1.0 - corr_block) * (1.0 - corr_block), OFF_WEIGHT * corr_block * corr_block
    )
    kernel = jnp.where(on_diag, corr_block - 1.0, OFF_WEIGHT * corr_block).astype(jnp.bfloat16)
    return (kernel, jnp.sum(terms))


def body(table, text, table_proj, text_proj):
    full_table, full_text = (
        lax.all_gather(table, "feat", axis=1, tiled=True),
        lax.all_gather(text, "feat", axis=1, tiled=True),
    )
    z_table = jnp.dot(full_table, table_proj, preferred_element_type=jnp.float32)
    z_text = jnp.dot(full_text, text_proj, preferred_element_type=jnp.float32)
    sum_table, sq_table, sum_text, sq_text = lax.psum(
        (
            jnp.sum(z_table, axis=0),
            jnp.sum(z_table * z_table, axis=0),
            jnp.sum(z_text, axis=0),
            jnp.sum(z_text * z_text, axis=0),
        ),
        "dp",
    )
    num_dp = lax.axis_size("dp")
    local_rows = z_table.shape[0]
    pairs = local_rows * num_dp
    normed_table, inverse_table = normalize(z_table, sum_table, sq_table, pairs)
    normed_text, inverse_text = normalize(z_text, sum_text, sq_text, pairs)
    half_table = normed_table.astype(jnp.bfloat16)
    half_text = normed_text.astype(jnp.bfloat16)
    text_full = lax.all_gather(half_text, "feat", axis=1, tiled=True)
    local_feats = half_table.shape[1]
    all_feats = text_full.shape[1]
    dp_index = lax.axis_index("dp")
    feat_index = lax.axis_index("feat")
    sub_width = all_feats // num_dp
    text_sub = lax.all_to_all(text_full, "dp", split_axis=1, concat_axis=0, tiled=True)
    corr_block = (
        lax.dot_general(
            lax.all_gather(half_table, "dp", axis=0, tiled=True),
            text_sub,
            (((0,), (0,)), ((), ())),
            preferred_element_type=jnp.float32,
        )
        / pairs
    )
    row_index = feat_index * local_feats + jnp.arange(local_feats, dtype=jnp.int32)
    col_index = dp_index * sub_width + jnp.arange(sub_width, dtype=jnp.int32)
    kernel, loss_part = kernel_block(corr_block, row_index, col_index)
    kernel_local = lax.all_gather(kernel, "dp", axis=1, tiled=True)
    loss_total = lax.psum(loss_part, ("dp", "feat"))
    loss_mean = (loss_total / all_feats).reshape(1)
    d_table = lax.dot_general(
        text_full, kernel_local, (((1,), (1,)), ((), ())), preferred_element_type=jnp.float32
    )
    text_terms = jnp.dot(half_table, kernel_local, preferred_element_type=jnp.float32)
    d_text = lax.psum_scatter(text_terms, "feat", scatter_dimension=1, tiled=True)
    mean_table, tilt_table, mean_text, tilt_text = lax.psum(
        (
            jnp.sum(d_table, axis=0),
            jnp.sum(d_table * normed_table, axis=0),
            jnp.sum(d_text, axis=0),
            jnp.sum(d_text * normed_text, axis=0),
        ),
        "dp",
    )
    back_table = (
        inverse_table * (d_table - mean_table / pairs - normed_table * (tilt_table / pairs))
    ).astype(jnp.bfloat16)
    back_text = (
        inverse_text * (d_text - mean_text / pairs - normed_text * (tilt_text / pairs))
    ).astype(jnp.bfloat16)
    table_terms = lax.dot_general(
        back_table, table_proj, (((1,), (1,)), ((), ())), preferred_element_type=jnp.float32
    )
    text_embed_terms = lax.dot_general(
        back_text, text_proj, (((1,), (1,)), ((), ())), preferred_element_type=jnp.float32
    )
    grad_table, grad_text = (
        lax.psum_scatter(table_terms, "feat", scatter_dimension=1, tiled=True),
        lax.psum_scatter(text_embed_terms, "feat", scatter_dimension=1, tiled=True),
    )
    return (grad_table, grad_text, loss_mean)


def solution(mesh):
    placed = (P("dp", "feat"), P("dp", "feat"), P(None, "feat"), P(None, "feat"))
    return jax.shard_map(
        body,
        mesh=mesh,
        in_specs=placed,
        out_specs=(P("dp", "feat"), P("dp", "feat"), P()),
        check_vma=False,
    )
```

profile of v0, /device:TPU:32, one launch (start us, length us, event | category | flops | bytes accessed | tf_op | source)
XLA Modules:
  0.0 739.9 jit_solution(3149157199122691087)
XLA Ops:
  7.2 0.0 all-gather.4.cloned.1.call-start
  7.2 0.0 copy-start
  7.2 47.9 %all_gather.15 = bf16[128,3584]{0,1:T(8,128)(2,1)S(1)} all-gather(bf16[128,448]{0,1:T(8,128)(2,1)} %param.4), channel_id=1, replica_groups=mesh['dp'=32,'feat'=8] {'feat'}, dimensions={1}, use_global_device_ids=true | all-gather | bytes 1032192 | tf_op jit(solution)/shard_map/all_gather | solution.py:28
  55.1 48.1 %all_gather.16 = bf16[128,3584]{0,1:T(8,128)(2,1)S(1)} all-gather(bf16[128,448]{0,1:T(8,128)(2,1)} %param.5), channel_id=1, replica_groups=mesh['dp'=32,'feat'=8] {'feat'}, dimensions={1}, use_global_device_ids=true | all-gather | bytes 1032192 | tf_op jit(solution)/shard_map/all_gather | solution.py:29
  103.2 2.7 multiply_reduce_fusion.3
  106.0 0.0 copy-done
  106.0 0.7 fusion.16
  106.7 54.0 %all-reduce.1 = (f32[512]{0:T(512)S(1)}, f32[512]{0:T(512)S(1)}, f32[512]{0:T(512)S(1)}, f32[512]{0:T(512)S(1)}) all-reduce(f32[512]{0:T(512)S(1)} %get-tuple-element.10, f32[512]{0:T(512)S(1)} %get-tuple-element.9, f32[512]{0:T(512)S(1)} %get-tuple-element.8, f32[512]{0:T(512)S(1)} %get-tuple-element.7), channel_id=1, replica_groups=mesh['dp'=32,'feat'=8] {'dp'}, use_global_device_ids=true, to_apply=%region_7.0 | all-reduce | flops 2048 | bytes 16384 | tf_op jit(solution)/shard_map/psum | solution.py:33
  160.7 0.7 fusion.2
  161.4 0.0 all-gather.4.cloned.1.call-update
  161.4 0.0 all-gather.6.cloned.1.call-start
  161.4 0.7 fusion.3
  162.1 0.0 all-gather.6.cloned.1.call-update
  162.2 71.8 %all-gather.4.cloned.1.call-done = bf16[128,4096]{1,0:T(8,128)(2,1)} async-done(((bf16[128,512]{1,0:T(8,128)(2,1)}), bf16[128,4096]{1,0:T(8,128)(2,1)}) %all-gather.4.cloned.1.call-update) | async-done | bytes 1048592 | tf_op jit(solution)/shard_map/all_gather | solution.py:49
  234.0 2.5 copy_bitcast_fusion
  236.5 5.9 all-to-all-start
  242.4 0.0 copy-start.2
  242.4 0.0 all-gather.8.cloned.1.call-start
  242.5 32.9 %all-to-all-done = bf16[128,32,128]{2,0,1:T(8,128)(2,1)S(1)} async-done(((bf16[128,32,128]{2,0,1:T(8,128)(2,1)}), bf16[128,32,128]{2,0,1:T(8,128)(2,1)S(1)}, u32[]{:S(2)}, u32[]{:S(2)}) %all-to-all-start) | async-done | bytes 1048608 | tf_op jit(solution)/shard_map/all_to_all | solution.py:55
  275.4 29.8 %all-gather.6.cloned.1.call-done = bf16[4096,512]{1,0:T(8,128)(2,1)} async-done(((bf16[128,512]{1,0:T(8,128)(2,1)}), bf16[4096,512]{1,0:T(8,128)(2,1)}) %all-gather.6.cloned.1.call-update) | async-done | bytes 4194320 | tf_op jit(solution)/shard_map/all_gather | solution.py:58
  305.1 4.7 fusion.1
  309.9 0.0 all-gather.8.cloned.1.call-update
  309.9 0.0 copy-start.1
  309.9 0.0 reduce-scatter.6.cloned.1.call-start
  310.0 68.5 %all-gather.8.cloned.1.call-done = bf16[512,4096]{1,0:T(8,128)(2,1)} async-done(((bf16[512,128]{1,0:T(8,128)(2,1)}), bf16[512,4096]{1,0:T(8,128)(2,1)}) %all-gather.8.cloned.1.call-update) | async-done | bytes 4194320 | tf_op jit(solution)/shard_map/all_gather | solution.py:68
  378.5 0.0 copy-done.2
  378.5 4.2 fusion.17
  382.7 0.0 reduce-scatter.6.cloned.1.call-update
  382.7 0.0 reduce-scatter.8.cloned.1.call-start
  382.8 0.0 copy-done.1
  382.8 3.7 fusion.15
  386.5 91.0 %reduce-scatter.6.cloned.1.call-done = f32[128,512]{1,0:T(8,128)} async-done(((f32[128,4096]{1,0:T(8,128)}), f32[128,512]{1,0:T(8,128)}) %reduce-scatter.6.cloned.1.call-update) | async-done | bytes 262160 | tf_op jit(solution)/shard_map/reduce_scatter | solution.py:75
  477.5 1.0 fusion.14
  478.5 55.6 %all-reduce = (f32[512]{0:T(512)S(1)}, f32[512]{0:T(512)S(1)}, f32[512]{0:T(512)S(1)}, f32[512]{0:T(512)S(1)}) all-reduce(f32[512]{0:T(512)S(1)} %get-tuple-element.6, f32[512]{0:T(512)S(1)} %get-tuple-element.5, f32[512]{0:T(512)S(1)} %get-tuple-element.4, f32[512]{0:T(512)S(1)} %get-tuple-element.3), channel_id=1, replica_groups=mesh['dp'=32,'feat'=8] {'dp'}, use_global_device_ids=true, to_apply=%region_11.12 | all-reduce | flops 2048 | bytes 16384 | tf_op jit(solution)/shard_map/psum | solution.py:76
  534.2 4.5 fusion.5
  538.7 0.0 reduce-scatter.8.cloned.1.call-update
  538.7 0.0 reduce-scatter.4.cloned.1.call-start
  538.8 4.4 fusion.4
  543.2 0.0 reduce-scatter.4.cloned.1.call-update
  543.2 89.8 %psum.71 = f32[]{:T(128)} all-reduce(f32[]{:T(128)} %get-tuple-element.19), channel_id=1, replica_groups=mesh['dp'=32,'feat'=8] {'dp','feat'}, use_global_device_ids=true, to_apply=%region_20.21 | all-reduce | flops 1 | bytes 8 | tf_op jit(solution)/shard_map/psum | solution.py:69
  633.7 4.6 reduce-scatter.8.cloned.1.call-done
  638.3 93.6 %reduce-scatter.4.cloned.1.call-done = f32[128,448]{0,1:T(8,128)} async-done(((f32[128,3584]{0,1:T(8,128)}), f32[128,448]{0,1:T(8,128)}) %reduce-scatter.4.cloned.1.call-update) | async-done | bytes 229392 | tf_op jit(solution)/shard_map/reduce_scatter | solution.py:98
  (6 shorter events, 0.0 us)
Async XLA Ops:
  7.2 226.8 %all-gather.4.cloned.1.call-start = ((), (), s32[]{:S(2)}) async-start(), calls=%async_computation.4 | async-start | bytes 1179648 | tf_op jit(solution)/shard_map/all_gather | solution.py:49
  7.2 98.7 %copy-start = (bf16[3584,512]{1,0:T(8,128)(2,1)S(1)}, bf16[3584,512]{1,0:T(8,128)(2,1)}, u32[]{:S(2)}) copy-start(bf16[3584,512]{1,0:T(8,128)(2,1)} %param.7) | copy-start | bytes 11010052
  161.4 143.8 %all-gather.6.cloned.1.call-start = ((), (), s32[]{:S(2)}) async-start(), calls=%async_computation.5 | async-start | bytes 4325376 | tf_op jit(solution)/shard_map/all_gather | solution.py:58
  236.5 38.9 %all-to-all-start = ((bf16[128,32,128]{2,0,1:T(8,128)(2,1)}), bf16[128,32,128]{2,0,1:T(8,128)(2,1)S(1)}, u32[]{:S(2)}, u32[]{:S(2)}) async-start(bf16[128,32,128]{2,0,1:T(8,128)(2,1)} %copy_bitcast_fusion), calls=%async_computation | async-start | bytes 2097152 | tf_op jit(solution)/shard_map/all_to_all | solution.py:55
  242.4 136.1 %copy-start.2 = (bf16[128,512]{1,0:T(8,128)(2,1)S(1)}, bf16[128,512]{1,0:T(8,128)(2,1)}, u32[]{:S(2)}) copy-start(bf16[128,512]{1,0:T(8,128)(2,1)} %fusion.3) | copy-start | bytes 393220
  242.4 136.1 %all-gather.8.cloned.1.call-start = ((), (), s32[]{:S(2)}) async-start(), calls=%async_computation.6 | async-start | bytes 4325376 | tf_op jit(solution)/shard_map/all_gather | solution.py:68
  309.9 72.9 %copy-start.1 = (bf16[128,4096]{1,0:T(8,128)(2,1)S(1)}, bf16[128,4096]{1,0:T(8,128)(2,1)}, u32[]{:S(2)}) copy-start(bf16[128,4096]{1,0:T(8,128)(2,1)} %all-gather.4.cloned.1.call-done) | copy-start | bytes 3145732
  309.9 167.6 %reduce-scatter.6.cloned.1.call-start = ((), (), s32[]{:S(2)}) async-start(), calls=%async_computation.8 | async-start | bytes 2359296 | tf_op jit(solution)/shard_map/reduce_scatter | solution.py:75
  382.7 255.6 %reduce-scatter.8.cloned.1.call-start = ((), (), s32[]{:S(2)}) async-start(), calls=%async_computation.9 | async-start | bytes 2064384 | tf_op jit(solution)/shard_map/reduce_scatter | solution.py:99
  538.7 193.2 %reduce-scatter.4.cloned.1.call-start = ((), (), s32[]{:S(2)}) async-start(), calls=%async_computation.7 | async-start | bytes 2064384 | tf_op jit(solution)/shard_map/reduce_scatter | solution.py:98
Sparse Core Ops, SparseCore 0:
  161.5 72.4 all-gather.3
  236.4 68.7 all-gather.5
  310.0 68.3 all-gather.7
  382.9 94.5 reduce-scatter.5
  538.8 99.4 reduce-scatter.7
  643.4 88.4 reduce-scatter.3
where the time goes:
time: 742 us; the launch traced here: 740 us
  waiting for transfers between devices  392 us (53%)
  blocking collectives  295 us (40%)
  matrix products  25.1 us (3%)
  between operations  16 us (2%)
    reduce_scatter x1, waiting for transfers between devices, body(): lax.psum_scatter(table_terms, 'feat', scatter_dimension=1, tiled=True)  93.6 us
    reduce_scatter x1, waiting for transfers between devices, body(): lax.psum_scatter(text_terms, 'feat', scatter_dimension=1, tiled=True)  91 us
    psum x1, blocking collectives, body(): loss_total = lax.psum(loss_part, ('dp', 'feat'))  89.8 us
    all_gather x1, waiting for transfers between devices, body(): text_full = lax.all_gather(half_text, 'feat', axis=1, tiled=True)  71.8 us
    all_gather x1, waiting for transfers between devices, body(): kernel_local = lax.all_gather(kernel, 'dp', axis=1, tiled=True)  68.5 us
    psum x1, blocking collectives, body(): lax.psum((jnp.sum(d_table, axis=0), jnp.sum(d_table * normed_table, axis=...  55.6 us
    psum x1, blocking collectives, body(): lax.psum((jnp.sum(z_table, axis=0), jnp.sum(z_table * z_table, axis=0), j...  54 us
    all_gather x1, blocking collectives, body(): lax.all_gather(text, 'feat', axis=1, tiled=True)  48.1 us
  transfers between devices with their start and end apart: 7, of which 7 were waited for; matrix products, arithmetic and copies ran while one was open for 2% of the time, Pallas kernels for 0%

commit v1 on v0

v1 whole, which is shorter than its diff:
```python
import jax
import jax.numpy as jnp
from jax import lax
from jax.experimental import pallas as pl
from jax.experimental.pallas import tpu as pltpu
from jax.sharding import PartitionSpec as P

OFF_WEIGHT = 0.1
EPS = 1e-05
MESH = pl.DeviceIdType.MESH
BF16, F32 = jnp.bfloat16, jnp.float32
NUM_DP, NUM_FEAT = 32, 8

SLOTS = {}


def _slots(name, count):
    SLOTS[name] = sum(n for _, n in SLOTS.values()), count


for _name, _count in (
    ("emb_z", 1), ("emb_x", 3), ("emb_zx", 3),
    ("st1_a", 7), ("st1_b", 3),
    ("txt_z", 1), ("txt_x", 3), ("txt_zx", 3), ("txt_a2a", 8),
    ("tab_l", 1), ("tab_y", 3), ("tab_ly", 3),
    ("corr_c", 1), ("corr_h", 1), ("ker_c", 1),
    ("dx_a2a", 7), ("dx_x", 8), ("dx_z", 1),
    ("dt_y", 3), ("dt_l", 1),
    ("st2_a", 7), ("st2_b", 3),
    ("gr_far", 3), ("gr_near", 3), ("gr_z", 1),
    ("loss_x", 3), ("loss_z", 1),
):
    _slots(_name, _count)
NUM_SLOTS = sum(n for _, n in SLOTS.values())


def slot(name, i=0):
    return SLOTS[name][0] + i


def matmul(a, b, dims):
    return lax.dot_general(a, b, ((dims[:1], dims[1:]), ((), ())), preferred_element_type=F32)


def kernel(
    table, text, tproj, xproj,
    grad_table, grad_text, loss_out,
    pt, px, emb, z, st_a, st_b, half_full, tab_g, txt_g,
    part, part_c, part_h, part_hr, ker,
    dxp, dx, dx_r, dx_far, dx_zr, dtp, dt_r, dt_far, dt_lr,
    gp, gr, g_own, g_far, g_zr, ls_x, ls_z,
    ssem, rsem, lsem,
):
    rows, width = table.shape
    feats = tproj.shape[1]
    pairs = rows * NUM_DP
    half = feats // 2
    dp, ft = lax.axis_index("dp"), lax.axis_index("feat")
    zl, y, c = dp // 8, (dp // 2) % 4, dp % 2
    h, l = zl // 2, zl % 2
    zh, x = ft // 4, ft % 4

    def device(zl_=zl, y_=y, c_=c, zh_=zh, x_=x):
        return {"dp": (zl_ * 4 + y_) * 2 + c_, "feat": zh_ * 4 + x_}

    z_peer = device(zh_=1 - zh)
    c_peer = device(c_=1 - c)
    l_peer = device(zl_=h * 2 + 1 - l)
    h_peer = device(zl_=(1 - h) * 2 + l)

    def x_peer(i):
        return device(x_=(x + i) % 4)

    def y_peer(i):
        return device(y_=(y + i) % 4)

    yc = [(dy, dc) for dy in range(4) for dc in range(2) if dy or dc]
    yl = [(dy, dl) for dy in range(4) for dl in range(2) if dy or dl]

    def yl_peer(dy, dl):
        return device(y_=(y + dy) % 4, zl_=h * 2 + (l + dl) % 2)

    started = []

    def send(src, dst, s, to, r=None):
        copy = pltpu.make_async_remote_copy(
            src_ref=src, dst_ref=dst, send_sem=ssem.at[s], recv_sem=rsem.at[s if r is None else r],
            device_id=to, device_id_type=MESH,
        )
        copy.start()
        return copy

    def post(src, dst, s, to):
        copy = send(src, dst, s, to)
        started.append(copy)
        return copy

    load_t = pltpu.make_async_copy(tproj, pt, lsem.at[0])
    load_x = pltpu.make_async_copy(xproj, px, lsem.at[1])
    load_t.start()
    load_x.start()

    barrier = pltpu.get_barrier_semaphore()
    greet = [z_peer] + [x_peer(i) for i in (1, 2, 3)]
    greet += [device(y_=(y + dy) % 4, c_=(c + dc) % 2) for dy, dc in yc]
    greet += [device(zl_=(zl + i) % 4) for i in (1, 2, 3)]
    greet += [yl_peer(dy, 1) for dy in (1, 2, 3)]
    for to in greet:
        pl.semaphore_signal(barrier, inc=1, device_id=to, device_id_type=MESH)
    emb[ft, 0] = table[...]
    emb[ft, 1] = text[...]
    pl.semaphore_wait(barrier, len(greet))

    def add_block(f, first=False):
        at = pl.ds(pl.multiple_of(f * width, 64), width)
        for side, proj in ((0, pt), (1, px)):
            term = matmul(emb[f, side], proj[at, :], (1, 0))
            z[side] = term if first else z[side] + term

    own = emb.at[ft]
    emb_z = post(own, own, slot("emb_z"), z_peer)
    emb_x = [post(own, own, slot("emb_x", i - 1), x_peer(i)) for i in (1, 2, 3)]
    load_t.wait()
    load_x.wait()
    add_block(ft, True)
    ft_z = (1 - zh) * 4 + x
    emb_z.wait_recv()
    far = emb.at[ft_z]
    emb_zx = [post(far, far, slot("emb_zx", i - 1), x_peer(i)) for i in (1, 2, 3)]
    add_block(ft_z)
    for i in (1, 3, 2):
        emb_x[i - 1].wait_recv()
        add_block(zh * 4 + (x + 4 - i) % 4)
    for i in (1, 3, 2):
        emb_zx[i - 1].wait_recv()
        add_block((1 - zh) * 4 + (x + 4 - i) % 4)

    def sum_dp(k, value):
        a, b = st_a.at[k], st_b.at[k]
        me_a, me_b = y * 2 + c, zl
        a[me_a] = value
        copies = [
            post(a.at[me_a], a.at[me_a], slot("st%d_a" % (k + 1), j),
                 device(y_=(y + dy) % 4, c_=(c + dc) % 2))
            for j, (dy, dc) in enumerate(yc)
        ]
        for copy in copies:
            copy.wait_recv()
        b[me_b] = jnp.sum(a[...], axis=0)
        copies = [
            post(b.at[me_b], b.at[me_b], slot("st%d_b" % (k + 1), i - 1), device(zl_=(zl + i) % 4))
            for i in (1, 2, 3)
        ]
        for copy in copies:
            copy.wait_recv()
        return jnp.sum(b[...], axis=0)

    def column(v):
        return jnp.sum(v, axis=0, keepdims=True)

    zero = jnp.zeros((4, feats), F32)
    zt, zx = z[0], z[1]
    total = sum_dp(0, jnp.concatenate(
        [column(zt), column(zt * zt), column(zx), column(zx * zx), zero], axis=0))
    inverse = []
    for side in (0, 1):
        center = total[2 * side:2 * side + 1] / pairs
        spread = total[2 * side + 1:2 * side + 2] / pairs - center * center
        inv = lax.rsqrt(spread + EPS)
        z[side] = (z[side] - center) * inv
        inverse.append(inv)
    me_p, me_g = y * 2 + l, l * 4 + y

    tab_g[me_p] = z[0].astype(BF16)
    half_full[ft] = z[1].astype(BF16)

    def a2a(f, j, go):
        local = jnp.logical_and(f % 4 == y, f // 4 == l)
        copy = pltpu.make_async_remote_copy(
            src_ref=half_full.at[f], dst_ref=txt_g.at[me_p],
            send_sem=ssem.at[slot("txt_a2a", j)], recv_sem=rsem.at[slot("txt_a2a") + me_p],
            device_id=device(y_=f % 4, zl_=h * 2 + f // 4), device_id_type=MESH,
        )

        @pl.when(jnp.logical_not(local))
        def _():
            if go:
                copy.start()
            else:
                copy.wait_send()

        if go:
            @pl.when(local)
            def _():
                txt_g[me_p] = half_full[f]

    own = half_full.at[ft]
    far = half_full.at[ft_z]
    txt_z = post(own, own, slot("txt_z"), z_peer)
    txt_x = [post(own, own, slot("txt_x", i - 1), x_peer(i)) for i in (1, 2, 3)]
    mine = tab_g.at[me_p]
    tab_l = post(mine, mine, slot("tab_l"), l_peer)
    tab_y = [post(mine, mine, slot("tab_y", i - 1), y_peer(i)) for i in (1, 2, 3)]
    order = [ft]
    a2a(ft, 0, True)
    txt_z.wait_recv()
    txt_zx = [post(far, far, slot("txt_zx", i - 1), x_peer(i)) for i in (1, 2, 3)]
    a2a(ft_z, 1, True)
    order.append(ft_z)
    tab_l.wait_recv()
    other = tab_g.at[y * 2 + 1 - l]
    tab_ly = [post(other, other, slot("tab_ly", i - 1), y_peer(i)) for i in (1, 2, 3)]
    for copies, zz in ((txt_x, zh), (txt_zx, 1 - zh)):
        for i in (1, 3, 2):
            copies[i - 1].wait_recv()
            f = zz * 4 + (x + 4 - i) % 4
            a2a(f, len(order), True)
            order.append(f)
    for copy in tab_y + tab_ly:
        copy.wait_recv()
    for j in range(1, 8):
        s = (me_p + j) % 8
        pltpu.make_async_remote_copy(
            src_ref=txt_g.at[s], dst_ref=txt_g.at[s], send_sem=ssem.at[slot("txt_a2a")],
            recv_sem=rsem.at[slot("txt_a2a") + s], device_id=l_peer, device_id_type=MESH,
        ).wait_recv()

    group = 8 * rows
    part[...] = matmul(tab_g[...].reshape(group, feats), txt_g[...].reshape(group, feats), (0, 0))
    at_c = pl.ds(pl.multiple_of((1 - c) * half, half), half)
    me_c = pl.ds(pl.multiple_of(c * half, half), half)
    post(part.at[at_c], part_c, slot("corr_c"), c_peer).wait_recv()
    row_index = ft * feats + c * half + lax.broadcasted_iota(jnp.int32, (half, feats), 0)
    col_index = me_g * feats + lax.broadcasted_iota(jnp.int32, (half, feats), 1)
    on_diag = row_index == col_index
    less = (part[me_c, :] + part_c[...]) / pairs - jnp.where(on_diag, 0.5, 0.0)
    part_h[...] = less.astype(BF16)
    part_c[...] = less
    post(part_h, part_hr, slot("corr_h"), h_peer).wait_recv()
    less = part_c[...] + part_hr[...].astype(F32)
    weighed = jnp.where(on_diag, less, OFF_WEIGHT * less)
    ker[me_c, :] = weighed.astype(BF16)
    ker_c = post(ker.at[me_c], ker.at[me_c], slot("ker_c"), c_peer)
    loss_part = 0.5 * column(weighed * less)
    ker_c.wait_recv()

    dxp[...] = matmul(tab_g[...].reshape(group, feats), ker[...], (1, 0)).astype(BF16).reshape(
        8, rows, feats)
    dx_a2a = [
        post(dxp.at[((y + dy) % 4) * 2 + (l + dl) % 2], dx.at[me_g], slot("dx_a2a", j), yl_peer(dy, dl))
        for j, (dy, dl) in enumerate(yl)
    ]
    dx[me_g] = dxp[me_p]

    def dx_on(g, j, go):
        copy = pltpu.make_async_remote_copy(
            src_ref=dx.at[g], dst_ref=dx_r.at[g // 4, x], send_sem=ssem.at[slot("dx_x", j)],
            recv_sem=rsem.at[slot("dx_x") + (g // 4) * 4 + x],
            device_id=device(x_=g % 4), device_id_type=MESH,
        )

        @pl.when(g % 4 != x)
        def _():
            if go:
                copy.start()
            else:
                copy.wait_send()

        if go:
            @pl.when(g % 4 == x)
            def _():
                dx_r[g // 4, x] = dx[g]

    dx_order = [me_g]
    dx_on(me_g, 0, True)

    dtp[...] = matmul(txt_g[...].reshape(group, feats), ker[...], (1, 1)).astype(BF16).reshape(
        8, rows, feats)
    dt_y = [
        post(dtp.at[pl.ds(((y + i) % 4) * 2, 2)], dt_r.at[i - 1], slot("dt_y", i - 1), y_peer(i))
        for i in (1, 2, 3)
    ]
    for j, (dy, dl) in enumerate(yl):
        dx_a2a[j].wait_recv()
        g = ((l + dl) % 2) * 4 + (y + 4 - dy) % 4
        dx_on(g, j + 1, True)
        dx_order.append(g)

    def dx_sum(zz):
        for i in (1, 2, 3):
            s = (x + i) % 4
            pltpu.make_async_remote_copy(
                src_ref=dx_r.at[zz, s], dst_ref=dx_r.at[zz, s], send_sem=ssem.at[slot("dx_x")],
                recv_sem=rsem.at[slot("dx_x") + zz * 4 + s], device_id=z_peer, device_id_type=MESH,
            ).wait_recv()
        return jnp.sum(dx_r[zz].astype(F32), axis=0)

    dx_far[...] = dx_sum(1 - zh).astype(BF16)
    dx_z = post(dx_far, dx_zr, slot("dx_z"), z_peer)

    for copy in dt_y:
        copy.wait_recv()

    def dt_sum(ll):
        total = dtp[y * 2 + ll].astype(F32)
        for i in range(3):
            total = total + dt_r[i, ll].astype(F32)
        return total

    dt_far[...] = dt_sum(1 - l).astype(BF16)
    dt_l = post(dt_far, dt_lr, slot("dt_l"), l_peer)
    d_table = dt_sum(l)
    d_text = dx_sum(zh)
    dt_l.wait_recv()
    d_table = d_table + dt_lr[...].astype(F32)
    dx_z.wait_recv()
    d_text = d_text + dx_zr[...].astype(F32)

    zt, zx = z[0], z[1]
    total = sum_dp(1, jnp.concatenate(
        [column(d_table), column(d_table * zt), column(d_text), column(d_text * zx),
         loss_part, zero[:3]], axis=0))
    back = []
    for side, d in ((0, d_table), (1, d_text)):
        mean = total[2 * side:2 * side + 1] / pairs
        tilt = total[2 * side + 1:2 * side + 2] / pairs
        back.append((inverse[side] * (d - mean - z[side] * tilt)).astype(BF16))

    ls_x[0] = jnp.broadcast_to(jnp.sum(total[4:5], axis=1, keepdims=True), (8, 128))
    ls_copies = [post(ls_x.at[0], ls_x.at[i], slot("loss_x", i - 1), x_peer(i)) for i in (1, 2, 3)]

    copies = {}
    for k, zz in ((0, 1 - zh), (1, zh)):
        for i in (1, 3, 2, 0):
            f = zz * 4 + (x + i) % 4
            at = pl.ds(pl.multiple_of(f * width, 64), width)
            for side, proj in ((0, pt), (1, px)):
                term = matmul(back[side], proj[at, :], (1, 1))
                if i:
                    gp[k, i - 1, side] = term.astype(BF16)
                else:
                    g_own[k, side] = term
            if i:
                copies[k, i] = post(
                    gp.at[k, i - 1], gr.at[k, i - 1],
                    slot("gr_far" if k == 0 else "gr_near", i - 1), x_peer(i))

    def gr_sum(k, side):
        total = g_own[k, side]
        for i in range(3):
            total = total + gr[k, i, side].astype(F32)
        return total

    for copy in ls_copies:
        copy.wait_recv()
    ls_z[0] = jnp.sum(ls_x[...], axis=0)
    ls_copy = post(ls_z.at[0], ls_z.at[1], slot("loss_z"), z_peer)
    for i in (1, 3, 2):
        copies[0, i].wait_recv()
    for side in (0, 1):
        g_far[side] = gr_sum(0, side).astype(BF16)
    gr_z = post(g_far, g_zr, slot("gr_z"), z_peer)
    ls_copy.wait_recv()
    loss_out[...] = (ls_z[0] + ls_z[1]) / (feats * NUM_FEAT)
    for i in (1, 3, 2):
        copies[1, i].wait_recv()
    gr_z.wait_recv()
    grad_table[...] = gr_sum(1, 0) + g_zr[0].astype(F32)
    grad_text[...] = gr_sum(1, 1) + g_zr[1].astype(F32)

    for copy in started:
        copy.wait_send()
    for j, f in enumerate(order):
        a2a(f, j, False)
    for j, g in enumerate(dx_order):
        dx_on(g, j, False)


def body(table, text, table_proj, text_proj):
    rows, width = table.shape
    depth, feats = table_proj.shape
    half = feats // 2
    vmem = pl.BlockSpec(memory_space=pltpu.VMEM)
    hbm = pl.BlockSpec(memory_space=pl.ANY)
    v = pltpu.VMEM
    grad_table, grad_text, loss = pl.pallas_call(
        kernel,
        out_shape=(
            jax.ShapeDtypeStruct((rows, width), F32),
            jax.ShapeDtypeStruct((rows, width), F32),
            jax.ShapeDtypeStruct((8, 128), F32),
        ),
        in_specs=[vmem, vmem, hbm, hbm],
        out_specs=(vmem, vmem, vmem),
        scratch_shapes=[
            v((depth, feats), BF16), v((depth, feats), BF16),
            v((NUM_FEAT, 2, rows, width), BF16),
            v((2, rows, feats), F32),
            v((2, 8, 8, feats), F32), v((2, 4, 8, feats), F32),
            v((NUM_FEAT, rows, feats), BF16),
            v((8, rows, feats), BF16), v((8, rows, feats), BF16),
            v((feats, feats), F32), v((half, feats), F32),
            v((half, feats), BF16), v((half, feats), BF16),
            v((feats, feats), BF16),
            v((8, rows, feats), BF16), v((8, rows, feats), BF16),
            v((2, 4, rows, feats), BF16),
            v((rows, feats), BF16), v((rows, feats), BF16),
            v((8, rows, feats), BF16), v((3, 2, rows, feats), BF16),
            v((rows, feats), BF16), v((rows, feats), BF16),
            v((2, 3, 2, rows, width), BF16), v((2, 3, 2, rows, width), BF16),
            v((2, 2, rows, width), F32),
            v((2, rows, width), BF16), v((2, rows, width), BF16),
            v((4, 8, 128), F32), v((2, 8, 128), F32),
            pltpu.SemaphoreType.DMA((NUM_SLOTS,)),
            pltpu.SemaphoreType.DMA((NUM_SLOTS,)),
            pltpu.SemaphoreType.DMA((2,)),
        ],
        compiler_params=pltpu.CompilerParams(
            collective_id=0, has_side_effects=True, vmem_limit_bytes=56 * 1024 * 1024
        ),
        cost_estimate=pl.CostEstimate(flops=3_500_000_000, bytes_accessed=9_000_000, transcendentals=2048),
        name="barlow_step",
    )(table, text, table_proj, text_proj)
    return (grad_table, grad_text, loss[0, :1])


def solution(mesh):
    placed = (P("dp", "feat"), P("dp", "feat"), P(None, "feat"), P(None, "feat"))
    return jax.shard_map(
        body,
        mesh=mesh,
        in_specs=placed,
        out_specs=(P("dp", "feat"), P("dp", "feat"), P()),
        check_vma=False,
    )
```

time: 742 us -> 171 us (0.23)
  waiting for transfers between devices: 392 us -> 0 us
  blocking collectives: 295 us -> 0 us
  Pallas kernels: 0 us -> 162 us
  matrix products: 25.1 us -> 0 us
  between operations: 16 us -> 0.64 us
    psum x3 -> x0, blocking collectives: 199 us -> none  [the longest x1 89.8 us: body(): loss_total = lax.psum(loss_part, ('dp', 'feat'))]
    reduce_scatter x3 -> x0, waiting for transfers between devices: 189 us -> none  [the longest x1 93.6 us: body(): lax.psum_scatter(table_terms, 'feat', scatter_dimension=1, tiled=True)]
    all_gather x3 -> x0, waiting for transfers between devices: 170 us -> none  [the longest x1 71.8 us: body(): text_full = lax.all_gather(half_text, 'feat', axis=1, tiled=True)]
    pallas_call x0 -> x1, Pallas kernels: none -> 162 us  [body(): pl.pallas_call(kernel, out_shape=(jax.ShapeDtypeStruct((rows, width), F32...]
    all_gather x2 -> x0, blocking collectives: 96 us -> none  [the longest x1 48.1 us: body(): lax.all_gather(text, 'feat', axis=1, tiled=True)]
    all_to_all x1 -> x0, waiting for transfers between devices: 32.9 us -> none  [body(): lax.all_to_all(text_full, 'dp', split_axis=1, concat_axis=0, tiled=True)]
    dot_general x7 -> x0, matrix products: 25.1 us -> none  [the longest x1 4.74 us: body(): lax.dot_general(lax.all_gather(half_table, 'dp', axis=0, tiled=True), tex...]
  transfers between devices with their start and end apart: 7 -> 0, of which waited for: 7 -> 0; matrix products, arithmetic and copies ran while one was open for 2% -> 0% of each run, Pallas kernels for 0% -> 0%
where the time goes in v1:
time: 171 us
  Pallas kernels  162 us (95%)
  local copies, waits for them, and re-layouts  8.04 us (5%)
    pallas_call x1, Pallas kernels, body(): pl.pallas_call(kernel, out_shape=(jax.ShapeDtypeStruct((rows, width), F32...  162 us
    unnamed x4, local copies, waits for them, and re-layouts  6.86 us

profile of v1, /device:TPU:32, one launch (start us, length us, event | category | flops | bytes accessed | tf_op | source)
XLA Modules:
  0.0 170.5 jit_solution(18178264980928414936)
XLA Ops:
  0.6 1.7 copy.7.table
  2.3 1.7 copy.8.text
  3.9 161.9 %barlow_step.1 = (f32[128,448]{1,0:T(8,128)}, f32[128,448]{1,0:T(8,128)}, f32[8,128]{1,0:T(8,128)}) custom-call(bf16[128,448]{1,0:T(8,128)(2,1)} %copy.7.table, bf16[128,448]{1,0:T(8,128)(2,1)} %copy.8.text, bf16[3584,512]{1,0:T(8,128)(2,1)} %tproj.1, bf16[3584,512]{1,0:T(8,128)(2,1)} %xproj.1), custom_call_target="tpu_custom_call" | custom-call | flops 3500000000 | bytes 9000000 | tf_op jit(solution)/shard_map/barlow_step/pallas_call | solution.py:386
  165.8 1.2 slice.3
  167.0 1.8 %copy.9 = f32[128,448]{0,1:T(8,128)} copy(f32[128,448]{1,0:T(8,128)} %get-tuple-element.9) | data formatting | bytes 458752
  168.8 1.8 %copy.10 = f32[128,448]{0,1:T(8,128)} copy(f32[128,448]{1,0:T(8,128)} %get-tuple-element.10) | data formatting | bytes 458752

commit v2 on v0

v2 whole, which is shorter than its diff:
```python
import jax
import jax.numpy as jnp
from jax import lax
from jax.experimental import pallas as pl
from jax.experimental.pallas import tpu as pltpu
from jax.sharding import PartitionSpec as P

OFF_WEIGHT = 0.1
EPS = 1e-05
MESH = pl.DeviceIdType.MESH
BF16, F32 = jnp.bfloat16, jnp.float32
NUM_DP, NUM_FEAT = 32, 8
TABLE, TEXT = 0, 1
FAR, NEAR = 0, 1
LANES = 128

SLOTS = {}
for _name, _count in (
    ("emb_z", 2), ("emb_x", 16),
    ("st_a", 28), ("st_b", 12),
    ("txt_z", 1), ("txt_x", 8), ("txt_a2a", 8),
    ("tab_c", 4), ("tab_y", 4),
    ("corr_l", 2), ("corr_h", 2), ("ker_l", 2),
    ("dx_a2a", 16), ("dx_x", 12), ("dx_z", 2),
    ("dt_y", 6), ("dt_c", 1),
    ("gr_x", 24), ("gr_z", 2),
    ("loss_x", 3), ("loss_z", 1),
):
    SLOTS[_name] = (sum(n for _, n in SLOTS.values()), _count)
NUM_SLOTS = sum(n for _, n in SLOTS.values())


def slot(name, i=0):
    return SLOTS[name][0] + i


def matmul(a, b, dims):
    return lax.dot_general(a, b, ((dims[:1], dims[1:]), ((), ())), preferred_element_type=F32)


def column(v):
    return jnp.sum(v, axis=0, keepdims=True)


def fold(v):
    n = v.shape[1] // LANES
    return jnp.concatenate([v[:, i * LANES:(i + 1) * LANES] for i in range(n)], axis=0)


def unfold(v):
    return jnp.concatenate([v[i:i + 1] for i in range(v.shape[0])], axis=1)


class Gather:
    def __init__(self, post, base, peer, block):
        self.post, self.base, self.peer, self.block = post, base, peer, block

    def start(self):
        own = self.block(0)
        self.from_left = self.post(own, own, self.base, self.peer(1))
        self.from_right = self.post(own, own, self.base + 1, self.peer(3))

    def relay_left(self):
        self.from_left.wait_recv()
        part = self.block(3, 0)
        self.half_left = self.post(part, part, self.base + 2, self.peer(1))

    def relay_right(self):
        self.from_right.wait_recv()
        part = self.block(1, 1)
        self.half_right = self.post(part, part, self.base + 3, self.peer(3))

    def finish(self):
        self.half_left.wait_recv()
        self.half_right.wait_recv()


class Reduce:
    def __init__(self, post, base, peer, src, val, buf):
        self.post, self.base, self.peer, self.src, self.val, self.buf = post, base, peer, src, val, buf
        self.relayed, self.direct, self.final_copy = {}, {}, {}

    def send_opposite(self, half):
        to = (1, 3)[half]
        self.relayed[half] = self.post(
            self.src(2, half), self.buf.at[0, half], self.base + half, self.peer(to))

    def send_direct(self, half):
        to = (3, 1)[half]
        self.direct[half] = self.post(
            self.src(to, half), self.buf.at[1, half], self.base + 2 + half, self.peer(to))

    def pass_on(self, half):
        to = (1, 3)[half]
        self.relayed[half].wait_recv()
        self.buf[2, half] = (self.buf[0, half].astype(F32) + self.val(to, half)).astype(BF16)
        self.final_copy[half] = self.post(
            self.buf.at[2, half], self.buf.at[3, half], self.base + 4 + half, self.peer(to))

    def total(self, half):
        self.direct[half].wait_recv()
        self.final_copy[half].wait_recv()
        return self.val(0, half) + self.buf[1, half].astype(F32) + self.buf[3, half].astype(F32)


def kernel(
    table, text, tproj, xproj,
    grad_table, grad_text, loss_out,
    pt, px, emb, z, st_a, st_b, half_full, tab_g, txt_g,
    part, part_s, part_r, part_h, part_hr, ker,
    dxp, dx, dx_buf, dx_far, dx_zr, dtp, dt_cr, dt_half, dt_buf, d,
    gp, g_own, gr_buf, g_far, g_zr, ls_x, ls_z,
    ssem, rsem, lsem,
):
    width, rows = table.shape
    feats = tproj.shape[1]
    pairs = rows * NUM_DP
    half = feats // 2
    low, mid = rows // 2, width // 2
    projs = (pt, px)
    dp, ft = lax.axis_index("dp"), lax.axis_index("feat")
    zl, y, c = dp // 8, (dp // 2) % 4, dp % 2
    h, l = zl // 2, zl % 2
    zh, x = ft // 4, ft % 4
    me_p, me_g = y * 2 + c, c * 4 + y

    def device(zl_=zl, y_=y, c_=c, zh_=zh, x_=x):
        return {"dp": (zl_ * 4 + y_) * 2 + c_, "feat": zh_ * 4 + x_}

    z_peer = device(zh_=1 - zh)
    c_peer = device(c_=1 - c)
    l_peer = device(zl_=h * 2 + 1 - l)
    h_peer = device(zl_=(1 - h) * 2 + l)

    def x_peer(i):
        return device(x_=(x + i) % 4)

    def y_peer(i):
        return device(y_=(y + i) % 4)

    yc = [(dy, dc) for dy in range(4) for dc in range(2) if dy or dc]

    def yc_peer(dy, dc):
        return device(y_=(y + dy) % 4, c_=(c + dc) % 2)

    def zl_peer(i):
        return device(zl_=(zl + i) % 4)

    drain = []

    def remote(src, dst, s, to, r=None):
        return pltpu.make_async_remote_copy(
            src_ref=src, dst_ref=dst, send_sem=ssem.at[s], recv_sem=rsem.at[s if r is None else r],
            device_id=to, device_id_type=MESH,
        )

    def post(src, dst, s, to, r=None):
        copy = remote(src, dst, s, to, r)
        copy.start()
        drain.append(copy.wait_send)
        return copy

    loads = [
        pltpu.make_async_copy(a, b, lsem.at[i])
        for i, (a, b) in enumerate(
            ((table, emb.at[ft, TABLE]), (text, emb.at[ft, TEXT]), (tproj, pt), (xproj, px)))
    ]
    for i in (1, 0, 3, 2):
        loads[i].start()

    barrier = pltpu.get_barrier_semaphore()
    greet = [z_peer] + [x_peer(i) for i in (1, 2, 3)]
    greet += [yc_peer(*k) for k in yc] + [zl_peer(i) for i in (1, 2, 3)]
    for to in greet:
        pl.semaphore_signal(barrier, inc=1, device_id=to, device_id_type=MESH)
    loads[1].wait()
    loads[0].wait()
    pl.semaphore_wait(barrier, len(greet))

    def feat(zz, k):
        return zz * 4 + (x + k) % 4

    zf = 1 - zh
    ft_z = feat(zf, 0)

    def add_block(side, f, first=False):
        at = pl.ds(pl.multiple_of(f * width, 64), width)
        term = matmul(emb[f, side], projs[side][at, :], (0, 0))
        z[side] = term if first else z[side] + term

    def emb_gather(side, where):
        def block(k, part_=None):
            f = feat((zf, zh)[where], k)
            return emb.at[f, side] if part_ is None else emb.at[f, side, pl.ds(part_ * mid, mid)]

        return Gather(post, slot("emb_x", (side * 2 + where) * 4), x_peer, block)

    def emb_send_z(side):
        own = emb.at[ft, side]
        return post(own, own, slot("emb_z", side), z_peer)

    def emb_relay(g, side, zz):
        g.relay_left()
        g.relay_right()
        add_block(side, feat(zz, 3))
        add_block(side, feat(zz, 1))

    stats = {}

    def stat_a(k, value):
        n = value.shape[0]
        a = st_a.at[k, me_p, pl.ds(0, n)]
        a[...] = value
        stats[k, 0] = n, [
            post(a, a, slot("st_a", k * 7 + j), yc_peer(*to)) for j, to in enumerate(yc)]

    def stat_b(k):
        n, copies = stats[k, 0]
        for copy in copies:
            copy.wait_recv()
        b = st_b.at[k, zl, pl.ds(0, n)]
        b[...] = jnp.sum(st_a[k, :, :n], axis=0)
        stats[k, 1] = [
            post(b, b, slot("st_b", k * 3 + i - 1), zl_peer(i)) for i in (1, 2, 3)]

    def stat_c(k):
        for copy in stats[k, 1]:
            copy.wait_recv()
        return jnp.sum(st_b[k, :, :stats[k, 0][0]], axis=0)

    def forward_stats(side):
        v = z[side]
        stat_a(side, jnp.concatenate([fold(column(v)), fold(column(v * v))], axis=0))

    lanes = feats // LANES

    def forward_normalize(side):
        total = stat_c(side)
        center = unfold(total[:lanes]) / pairs
        spread = unfold(total[lanes:2 * lanes]) / pairs - center * center
        inv = lax.rsqrt(spread + EPS)
        z[side] = (z[side] - center) * inv
        return inv

    emb_zx = emb_send_z(TEXT)
    xn = emb_gather(TEXT, NEAR)
    xn.start()
    loads[3].wait()
    add_block(TEXT, ft, True)
    emb_zt = emb_send_z(TABLE)
    emb_relay(xn, TEXT, zh)
    emb_zx.wait_recv()
    xf = emb_gather(TEXT, FAR)
    xf.start()
    tn = emb_gather(TABLE, NEAR)
    tn.start()
    add_block(TEXT, ft_z)
    loads[2].wait()
    add_block(TABLE, ft, True)
    xn.finish()
    add_block(TEXT, feat(zh, 2))
    emb_relay(xf, TEXT, zf)
    emb_relay(tn, TABLE, zh)
    emb_zt.wait_recv()
    tf = emb_gather(TABLE, FAR)
    tf.start()
    add_block(TABLE, ft_z)
    xf.finish()
    add_block(TEXT, feat(zf, 2))
    forward_stats(TEXT)
    tn.finish()
    add_block(TABLE, feat(zh, 2))
    emb_relay(tf, TABLE, zf)
    stat_b(TEXT)
    tf.finish()
    add_block(TABLE, feat(zf, 2))
    forward_stats(TABLE)
    inv_text = forward_normalize(TEXT)

    half_full[ft] = z[TEXT].astype(BF16)

    def a2a(f, j):
        local = jnp.logical_and(f % 4 == y, f // 4 == c)
        copy = remote(
            half_full.at[f], txt_g.at[me_p], slot("txt_a2a", j),
            device(y_=f % 4, c_=f // 4), slot("txt_a2a") + me_p)

        @pl.when(jnp.logical_not(local))
        def _():
            copy.start()

        @pl.when(local)
        def _():
            txt_g[me_p] = half_full[f]

        def wait():
            @pl.when(jnp.logical_not(local))
            def _():
                copy.wait_send()

        drain.append(wait)

    def txt_gather(where):
        def block(k, part_=None):
            f = feat((zf, zh)[where], k)
            return half_full.at[f] if part_ is None else half_full.at[f, pl.ds(part_ * low, low)]

        return Gather(post, slot("txt_x", where * 4), x_peer, block)

    def tab_block(k, part_=None):
        p = ((y + k) % 4) * 2 + c
        return tab_g.at[p] if part_ is None else tab_g.at[p, pl.ds(part_ * low, low)]

    def tab_share(k):
        return post(tab_block(k), tab_block(k), slot("tab_c", k), c_peer)

    own = half_full.at[ft]
    txt_z = post(own, own, slot("txt_z"), z_peer)
    cn = txt_gather(NEAR)
    cn.start()
    a2a(ft, 0)
    stat_b(TABLE)
    cn.relay_left()
    a2a(feat(zh, 3), 1)
    cn.relay_right()
    a2a(feat(zh, 1), 2)
    inv_table = forward_normalize(TABLE)
    tab_g[me_p] = z[TABLE].astype(BF16)
    hn = Gather(post, slot("tab_y"), y_peer, tab_block)
    hn.start()
    shared = [tab_share(0)]
    txt_z.wait_recv()
    cf = txt_gather(FAR)
    cf.start()
    a2a(ft_z, 3)
    cn.finish()
    a2a(feat(zh, 2), 4)
    hn.relay_left()
    shared.append(tab_share(3))
    hn.relay_right()
    shared.append(tab_share(1))
    cf.relay_left()
    a2a(feat(zf, 3), 5)
    cf.relay_right()
    a2a(feat(zf, 1), 6)
    hn.finish()
    shared.append(tab_share(2))
    cf.finish()
    a2a(feat(zf, 2), 7)
    for copy in shared:
        copy.wait_recv()
    for j in range(1, 8):
        s = (me_p + j) % 8
        remote(txt_g.at[s], txt_g.at[s], slot("txt_a2a"), c_peer, slot("txt_a2a") + s).wait_recv()

    group = 8 * rows
    tabs = tab_g[...].reshape(group, feats)
    at_l = pl.ds(pl.multiple_of((1 - l) * half, half), half)
    me_l = pl.ds(pl.multiple_of(l * half, half), half)
    chunks = [slice(0, half), slice(half, feats)]
    corr_l = []
    for k, cols in enumerate(chunks):
        row_index = ft * feats + lax.broadcasted_iota(jnp.int32, (feats, half), 0)
        col_index = me_g * feats + k * half + lax.broadcasted_iota(jnp.int32, (feats, half), 1)
        part[k] = matmul(tabs, txt_g[:, :, cols].reshape(group, half), (0, 0)) / pairs - jnp.where(
            row_index == col_index, 0.25, 0.0)
        part_s[k] = part[k, at_l, :].astype(BF16)
        corr_l.append(post(part_s.at[k], part_r.at[k], slot("corr_l", k), l_peer))
    corr_h = []
    for k in (0, 1):
        corr_l[k].wait_recv()
        less = part[k, me_l, :] + part_r[k].astype(F32)
        part_h[k] = less.astype(BF16)
        part[k, me_l, :] = less
        corr_h.append(post(part_h.at[k], part_hr.at[k], slot("corr_h", k), h_peer))

    loss_part = None
    for k in (0, 1):
        corr_h[k].wait_recv()
        less = part[k, me_l, :] + part_hr[k].astype(F32)
        row_index = ft * feats + l * half + lax.broadcasted_iota(jnp.int32, (half, half), 0)
        col_index = me_g * feats + k * half + lax.broadcasted_iota(jnp.int32, (half, half), 1)
        weighed = jnp.where(row_index == col_index, less, OFF_WEIGHT * less)
        ker[k, me_l, :] = weighed.astype(BF16)
        mine = ker.at[k, me_l]
        ker_l = post(mine, mine, slot("ker_l", k), l_peer)
        loss_k = column(0.5 * weighed * less)
        loss_part = loss_k if loss_part is None else loss_part + loss_k
        ker_l.wait_recv()
        dxp[k] = matmul(tab_g[...].reshape(group, feats), ker[k], (1, 0)).astype(BF16).reshape(
            8, rows, half)
        for j, (dy, dc) in enumerate(yc):
            post(dxp.at[k, ((y + dy) % 4) * 2 + (c + dc) % 2], dx.at[k, me_g],
                 slot("dx_a2a", k * 8 + j), yc_peer(dy, dc), slot("dx_a2a") + k * 8 + me_g)
        dx[k, me_g] = dxp[k, me_p]

    def dx_wait(k, g):
        @pl.when(g != me_g)
        def _():
            remote(dx.at[k, g], dx.at[k, g], slot("dx_a2a"), z_peer, slot("dx_a2a") + k * 8 + g).wait_recv()

    txts = txt_g[...].reshape(group, feats)
    both = (
        matmul(txts[:, chunks[0]], ker[0], (1, 1)) + matmul(txts[:, chunks[1]], ker[1], (1, 1))
    ).reshape(4, 2, rows, feats)
    for k in (0, 1):
        dtp[k] = both[:, k]
    dt_c = post(dtp.at[1 - c], dt_cr, slot("dt_c"), c_peer)

    def dt_src(k, part_):
        return dt_half.at[(y + k) % 4, pl.ds(part_ * low, low)]

    def dt_val(k, part_):
        return dt_cr[(y + k) % 4, part_ * low:(part_ + 1) * low, :]

    dt = Reduce(post, slot("dt_y"), y_peer, dt_src, dt_val, dt_buf)

    def dt_start():
        dt_c.wait_recv()
        for k in (2, 3, 1, 0):
            at = (y + k) % 4
            total = dtp[c, at] + dt_cr[at]
            dt_cr[at] = total
            dt_half[at] = total.astype(BF16)
            if k == 2:
                dt.send_opposite(0)
                dt.send_opposite(1)
            elif k:
                dt.send_direct(0 if k == 3 else 1)

    def dx_reduce(where):
        def src(k, part_):
            return dx.at[part_, feat((zf, zh)[where], k)]

        return Reduce(post, slot("dx_x", where * 6), x_peer, src,
                      lambda k, part_: src(k, part_)[...].astype(F32), dx_buf.at[where])

    dxr = [dx_reduce(FAR), dx_reduce(NEAR)]
    for k in (0, 1):
        if k == 1:
            dt_start()
        for r, zz in zip(dxr, (zf, zh)):
            dx_wait(k, feat(zz, 2))
            r.send_opposite(k)
            dx_wait(k, feat(zz, (3, 1)[k]))
            r.send_direct(k)
        for r, zz in zip(dxr, (zf, zh)):
            dx_wait(k, feat(zz, (1, 3)[k]))
            r.pass_on(k)
            dx_wait(k, feat(zz, 0))
    dt.pass_on(0)
    dt.pass_on(1)
    dx_z = []
    for k in (0, 1):
        dx_far[k] = dxr[FAR].total(k).astype(BF16)
        dx_z.append(post(dx_far.at[k], dx_zr.at[k], slot("dx_z", k), z_peer))
    for k in (0, 1):
        d[TABLE, pl.ds(k * low, low)] = dt.total(k)

    def backward_stats(side, extra=None):
        v = d[side]
        parts = [fold(column(v)), fold(column(v * z[side]))]
        if extra is not None:
            parts += [fold(extra), jnp.zeros((lanes, LANES), F32)]
        stat_a(2 + side, jnp.concatenate(parts, axis=0))

    def backward(side, inv):
        total = stat_c(2 + side)
        mean = unfold(total[:lanes]) / pairs
        tilt = unfold(total[lanes:2 * lanes]) / pairs
        return (inv * (d[side] - mean - z[side] * tilt)).astype(BF16), total

    backward_stats(TABLE, loss_part)
    for k, cols in enumerate(chunks):
        v = dxr[NEAR].total(k)
        dx_z[k].wait_recv()
        d[TEXT, :, cols] = v + dx_zr[k].astype(F32)
    stat_b(2 + TABLE)
    backward_stats(TEXT)

    def grad_reduce(side, where):
        def src(k, part_):
            return gp.at[side, where, k, pl.ds(part_ * mid, mid)]

        def val(k, part_):
            return g_own[side, where, k, part_ * mid:(part_ + 1) * mid, :]

        return Reduce(post, slot("gr_x", (side * 2 + where) * 6), x_peer, src, val,
                      gr_buf.at[side, where])

    def grad_terms(side, where, back, r):
        for k in (2, 3, 1, 0):
            at = pl.ds(pl.multiple_of(feat((zf, zh)[where], k) * width, 64), width)
            term = matmul(projs[side][at, :], back, (1, 1))
            if k:
                gp[side, where, k] = term.astype(BF16)
            if k != 2:
                g_own[side, where, k] = term
            if k == 2:
                r.send_opposite(0)
                r.send_opposite(1)
            elif k:
                r.send_direct(0 if k == 3 else 1)

    gr = [[grad_reduce(s, w) for w in (FAR, NEAR)] for s in (TABLE, TEXT)]
    grad_z = [None, None]

    def grad_far(side):
        for k in (0, 1):
            g_far[side, pl.ds(k * mid, mid)] = gr[side][FAR].total(k).astype(BF16)
        grad_z[side] = post(g_far.at[side], g_zr.at[side], slot("gr_z", side), z_peer)

    def grad_pass(side, where):
        gr[side][where].pass_on(0)
        gr[side][where].pass_on(1)

    back_table, total = backward(TABLE, inv_table)
    grad_terms(TABLE, FAR, back_table, gr[TABLE][FAR])
    stat_b(2 + TEXT)
    grad_terms(TABLE, NEAR, back_table, gr[TABLE][NEAR])
    ls_x[0] = jnp.broadcast_to(
        column(jnp.sum(total[2 * lanes:3 * lanes], axis=1, keepdims=True)), (8, LANES))
    ls_copies = [post(ls_x.at[0], ls_x.at[i], slot("loss_x", i - 1), x_peer(i)) for i in (1, 2, 3)]
    grad_pass(TABLE, FAR)
    back_text, _ = backward(TEXT, inv_text)
    grad_terms(TEXT, FAR, back_text, gr[TEXT][FAR])
    grad_far(TABLE)
    grad_pass(TABLE, NEAR)
    grad_terms(TEXT, NEAR, back_text, gr[TEXT][NEAR])
    grad_pass(TEXT, FAR)
    for copy in ls_copies:
        copy.wait_recv()
    ls_z[0] = jnp.sum(ls_x[...], axis=0)
    ls_copy = post(ls_z.at[0], ls_z.at[1], slot("loss_z"), z_peer)
    grad_far(TEXT)
    grad_pass(TEXT, NEAR)

    def grad_near(side, out):
        near = [gr[side][NEAR].total(k) for k in (0, 1)]
        grad_z[side].wait_recv()
        for k in (0, 1):
            at = slice(k * mid, (k + 1) * mid)
            out[at, :] = near[k] + g_zr[side, at, :].astype(F32)

    grad_near(TABLE, grad_table)
    ls_copy.wait_recv()
    loss_out[...] = ((ls_z[0] + ls_z[1]) / (feats * NUM_FEAT))[:1, :1]
    grad_near(TEXT, grad_text)
    for wait in drain:
        wait()


def body(table, text, table_proj, text_proj):
    rows, width = table.shape
    depth, feats = table_proj.shape
    half, low = feats // 2, rows // 2
    vmem = pl.BlockSpec(memory_space=pltpu.VMEM)
    hbm = pl.BlockSpec(memory_space=pl.ANY)
    v = pltpu.VMEM
    grad_table, grad_text, loss = pl.pallas_call(
        kernel,
        out_shape=(
            jax.ShapeDtypeStruct((width, rows), F32),
            jax.ShapeDtypeStruct((width, rows), F32),
            jax.ShapeDtypeStruct((1, 1), F32),
        ),
        in_specs=[hbm, hbm, hbm, hbm],
        out_specs=(vmem, vmem, vmem),
        scratch_shapes=[
            v((depth, feats), BF16), v((depth, feats), BF16),
            v((NUM_FEAT, 2, width, rows), BF16),
            v((2, rows, feats), F32),
            v((4, 8, 16, LANES), F32), v((4, 4, 16, LANES), F32),
            v((NUM_FEAT, rows, feats), BF16),
            v((8, rows, feats), BF16), v((8, rows, feats), BF16),
            v((2, feats, half), F32),
            v((2, half, half), BF16), v((2, half, half), BF16),
            v((2, half, half), BF16), v((2, half, half), BF16),
            v((2, feats, half), BF16),
            v((2, 8, rows, half), BF16), v((2, 8, rows, half), BF16),
            v((2, 4, 2, rows, half), BF16),
            v((2, rows, half), BF16), v((2, rows, half), BF16),
            v((2, 4, rows, feats), F32), v((4, rows, feats), F32),
            v((4, rows, feats), BF16), v((4, 2, low, feats), BF16),
            v((2, rows, feats), F32),
            v((2, 2, 4, width, rows), BF16), v((2, 2, 4, width, rows), F32),
            v((2, 2, 4, 2, width // 2, rows), BF16),
            v((2, width, rows), BF16), v((2, width, rows), BF16),
            v((4, 8, LANES), F32), v((2, 8, LANES), F32),
            pltpu.SemaphoreType.DMA((NUM_SLOTS,)),
            pltpu.SemaphoreType.DMA((NUM_SLOTS,)),
            pltpu.SemaphoreType.DMA((4,)),
        ],
        compiler_params=pltpu.CompilerParams(
            collective_id=0, has_side_effects=True, vmem_limit_bytes=56 * 1024 * 1024
        ),
        cost_estimate=pl.CostEstimate(flops=3_500_000_000, bytes_accessed=9_000_000, transcendentals=2048),
        name="barlow_step",
    )(table.T, text.T, table_proj, text_proj)
    return (grad_table.T, grad_text.T, loss.reshape(1))


def solution(mesh):
    placed = (P("dp", "feat"), P("dp", "feat"), P(None, "feat"), P(None, "feat"))
    return jax.shard_map(
        body,
        mesh=mesh,
        in_specs=placed,
        out_specs=(P("dp", "feat"), P("dp", "feat"), P()),
        check_vma=False,
    )
```

time: 742 us -> 142 us (0.19)
  waiting for transfers between devices: 392 us -> 0 us
  blocking collectives: 295 us -> 0 us
  Pallas kernels: 0 us -> 134 us
  matrix products: 25.1 us -> 0 us
  between operations: 16 us -> 2.46 us
    psum x3 -> x0, blocking collectives: 199 us -> none  [the longest x1 89.8 us: body(): loss_total = lax.psum(loss_part, ('dp', 'feat'))]
    reduce_scatter x3 -> x0, waiting for transfers between devices: 189 us -> none  [the longest x1 93.6 us: body(): lax.psum_scatter(table_terms, 'feat', scatter_dimension=1, tiled=True)]
    all_gather x3 -> x0, waiting for transfers between devices: 170 us -> none  [the longest x1 71.8 us: body(): text_full = lax.all_gather(half_text, 'feat', axis=1, tiled=True)]
    pallas_call x0 -> x1, Pallas kernels: none -> 134 us  [body(): pl.pallas_call(kernel, out_shape=(jax.ShapeDtypeStruct((width, rows), F32...]
    all_gather x2 -> x0, blocking collectives: 96 us -> none  [the longest x1 48.1 us: body(): lax.all_gather(text, 'feat', axis=1, tiled=True)]
    all_to_all x1 -> x0, waiting for transfers between devices: 32.9 us -> none  [body(): lax.all_to_all(text_full, 'dp', split_axis=1, concat_axis=0, tiled=True)]
    dot_general x7 -> x0, matrix products: 25.1 us -> none  [the longest x1 4.74 us: body(): lax.dot_general(lax.all_gather(half_table, 'dp', axis=0, tiled=True), tex...]
  transfers between devices with their start and end apart: 7 -> 0, of which waited for: 7 -> 0; matrix products, arithmetic and copies ran while one was open for 2% -> 0% of each run, Pallas kernels for 0% -> 0%
where the time goes in v2:
time: 142 us; the launch traced here: 140 us
  Pallas kernels  134 us (94%)
  local copies, waits for them, and re-layouts  3.28 us (2%)
  between operations  2.46 us (2%)
    pallas_call x1, Pallas kernels, body(): pl.pallas_call(kernel, out_shape=(jax.ShapeDtypeStruct((width, rows), F32...  134 us
    unnamed x2, local copies, waits for them, and re-layouts  3.28 us

profile of v2, /device:TPU:32, one launch (start us, length us, event | category | flops | bytes accessed | tf_op | source)
XLA Modules:
  0.0 140.2 jit_solution(73915704692998653)
XLA Ops:
  0.6 134.5 %barlow_step.1 = (f32[448,128]{1,0:T(8,128)}, f32[448,128]{1,0:T(8,128)}, f32[1,1]{1,0:T(1,128)}) custom-call(bf16[448,128]{1,0:T(8,128)(2,1)} %bitcast.7, bf16[448,128]{1,0:T(8,128)(2,1)} %bitcast.8, bf16[3584,512]{1,0:T(8,128)(2,1)} %tproj.1, bf16[3584,512]{1,0:T(8,128)(2,1)} %xproj.1), custom_call_target="tpu_custom_call" | custom-call | flops 3500000000 | bytes 9000000 | tf_op jit(solution)/shard_map/barlow_step/pallas_call | solution.py:560
  135.1 1.6 %copy.10 = f32[128,448]{0,1:T(8,128)} copy(f32[128,448]{0,1:T(8,128)} %bitcast.6) | data formatting | bytes 458752
  136.7 1.6 %copy.11 = f32[128,448]{0,1:T(8,128)} copy(f32[128,448]{0,1:T(8,128)} %bitcast.5) | data formatting | bytes 458752

commit v3 on v2

--- a/solution.py
+++ b/solution.py
@@ -11,17 +11,19 @@
 BF16, F32 = jnp.bfloat16, jnp.float32
 NUM_DP, NUM_FEAT = 32, 8
 TABLE, TEXT = 0, 1
+CHUNKS = 2
 FAR, NEAR = 0, 1
 LANES = 128
 
 SLOTS = {}
 for _name, _count in (
     ("emb_z", 2), ("emb_x", 16),
-    ("st_a", 28), ("st_b", 12),
+    ("st_a", 14), ("st_b", 6),
+    ("half_sum", 3), ("bt_a", 7), ("bt_b", 3), ("bx_l", 1), ("bx_x", 3), ("bx_z", 1), ("bx_y", 7),
     ("txt_z", 1), ("txt_x", 8), ("txt_a2a", 8),
     ("tab_c", 4), ("tab_y", 4),
-    ("corr_l", 2), ("corr_h", 2), ("ker_l", 2),
-    ("dx_a2a", 16), ("dx_x", 12), ("dx_z", 2),
+    ("corr_l", CHUNKS), ("corr_h", CHUNKS), ("ker_l", CHUNKS),
+    ("dx_a2a", CHUNKS * 8), ("dx_x", 12), ("dx_z", 2),
     ("dt_y", 6), ("dt_c", 1),
     ("gr_x", 24), ("gr_z", 2),
     ("loss_x", 3), ("loss_z", 1),
@@ -36,6 +38,16 @@
 
 def matmul(a, b, dims):
     return lax.dot_general(a, b, ((dims[:1], dims[1:]), ((), ())), preferred_element_type=F32)
+
+
+def split(v):
+    high = v.astype(BF16)
+    return high, (v - high.astype(F32)).astype(BF16)
+
+
+def rows_of(v):
+    high, low = split(v)
+    return jnp.concatenate([high, low, jnp.zeros((14, v.shape[1]), BF16)], axis=0)
 
 
 def column(v):
@@ -110,6 +122,7 @@
     part, part_s, part_r, part_h, part_hr, ker,
     dxp, dx, dx_buf, dx_far, dx_zr, dtp, dt_cr, dt_half, dt_buf, d,
     gp, g_own, gr_buf, g_far, g_zr, ls_x, ls_z,
+    halves, bt_a, bt_b, bx_l, bx_x, bx_z, bx_y,
     ssem, rsem, lsem,
 ):
     width, rows = table.shape
@@ -245,15 +258,15 @@
     emb_zx = emb_send_z(TEXT)
     xn = emb_gather(TEXT, NEAR)
     xn.start()
+    emb_zt = emb_send_z(TABLE)
+    tn = emb_gather(TABLE, NEAR)
+    tn.start()
     loads[3].wait()
     add_block(TEXT, ft, True)
-    emb_zt = emb_send_z(TABLE)
     emb_relay(xn, TEXT, zh)
     emb_zx.wait_recv()
     xf = emb_gather(TEXT, FAR)
     xf.start()
-    tn = emb_gather(TABLE, NEAR)
-    tn.start()
     add_block(TEXT, ft_z)
     loads[2].wait()
     add_block(TABLE, ft, True)
@@ -354,55 +367,88 @@
         remote(txt_g.at[s], txt_g.at[s], slot("txt_a2a"), c_peer, slot("txt_a2a") + s).wait_recv()
 
     group = 8 * rows
-    tabs = tab_g[...].reshape(group, feats)
+    wide = feats // CHUNKS
+    per_half = CHUNKS // 2
     at_l = pl.ds(pl.multiple_of((1 - l) * half, half), half)
     me_l = pl.ds(pl.multiple_of(l * half, half), half)
-    chunks = [slice(0, half), slice(half, feats)]
+    chunks = [slice(k * wide, (k + 1) * wide) for k in range(CHUNKS)]
+    halved = [slice(0, half), slice(half, feats)]
+    row_index = ft * feats + lax.broadcasted_iota(jnp.int32, (feats, feats), 0)
+    col_index = me_g * feats + lax.broadcasted_iota(jnp.int32, (feats, feats), 1)
+    part[...] = matmul(tab_g[...].reshape(group, feats), txt_g[...].reshape(group, feats), (0, 0)) / pairs - (
+        jnp.where(row_index == col_index, 0.25, 0.0))
     corr_l = []
     for k, cols in enumerate(chunks):
-        row_index = ft * feats + lax.broadcasted_iota(jnp.int32, (feats, half), 0)
-        col_index = me_g * feats + k * half + lax.broadcasted_iota(jnp.int32, (feats, half), 1)
-        part[k] = matmul(tabs, txt_g[:, :, cols].reshape(group, half), (0, 0)) / pairs - jnp.where(
-            row_index == col_index, 0.25, 0.0)
-        part_s[k] = part[k, at_l, :].astype(BF16)
+        part_s[k] = part[at_l, cols].astype(BF16)
         corr_l.append(post(part_s.at[k], part_r.at[k], slot("corr_l", k), l_peer))
+    sums = halves.at[zl]
+    sums[...] = jnp.concatenate(
+        [fold(column(jnp.sum(g[...].astype(F32), axis=0))) for g in (tab_g, txt_g)], axis=0)
+    half_sum = [post(sums, sums, slot("half_sum", i - 1), zl_peer(i)) for i in (1, 2, 3)]
     corr_h = []
-    for k in (0, 1):
+    for k, cols in enumerate(chunks):
         corr_l[k].wait_recv()
-        less = part[k, me_l, :] + part_r[k].astype(F32)
+        less = part[me_l, cols] + part_r[k].astype(F32)
         part_h[k] = less.astype(BF16)
-        part[k, me_l, :] = less
+        part[me_l, cols] = less
         corr_h.append(post(part_h.at[k], part_hr.at[k], slot("corr_h", k), h_peer))
 
-    loss_part = None
-    for k in (0, 1):
+    for copy in half_sum:
+        copy.wait_recv()
+    total = jnp.sum(halves[...], axis=0) / pairs
+    mean_tab, mean_txt = unfold(total[:lanes]), unfold(total[lanes:])
+    mean_tab = jnp.where(l == 0, mean_tab[:, :half], mean_tab[:, half:])
+    loss_part, tab_back, txt_back = None, None, []
+    ones = jnp.ones((16, wide), BF16)
+    tab_rows = rows_of(mean_tab)
+    for k, cols in enumerate(chunks):
         corr_h[k].wait_recv()
-        less = part[k, me_l, :] + part_hr[k].astype(F32)
-        row_index = ft * feats + l * half + lax.broadcasted_iota(jnp.int32, (half, half), 0)
-        col_index = me_g * feats + k * half + lax.broadcasted_iota(jnp.int32, (half, half), 1)
-        weighed = jnp.where(row_index == col_index, less, OFF_WEIGHT * less)
-        ker[k, me_l, :] = weighed.astype(BF16)
+        less = part[me_l, cols] + part_hr[k].astype(F32)
+        row_index = ft * feats + l * half + lax.broadcasted_iota(jnp.int32, (half, wide), 0)
+        col_index = me_g * feats + k * wide + lax.broadcasted_iota(jnp.int32, (half, wide), 1)
+        on_diag = row_index == col_index
+        weighed = jnp.where(on_diag, less, OFF_WEIGHT * less)
+        rounded = weighed.astype(BF16)
+        ker[k, me_l, :] = rounded
         mine = ker.at[k, me_l]
         ker_l = post(mine, mine, slot("ker_l", k), l_peer)
         loss_k = column(0.5 * weighed * less)
         loss_part = loss_k if loss_part is None else loss_part + loss_k
+        tilts = rounded.astype(F32) * jnp.where(on_diag, less + 1.0, less)
+        high, rest = split(tilts)
+        of_table = jnp.concatenate(
+            [(matmul(ones, high, (1, 1)) + matmul(ones, rest, (1, 1)))[:1],
+             column(matmul(rows_of(mean_txt[:, cols]), rounded, (1, 1)))], axis=0)
+        tab_back = of_table if tab_back is None else tab_back + of_table
+        txt_back.append((column(tilts), column(matmul(tab_rows, rounded, (1, 0)))))
         ker_l.wait_recv()
-        dxp[k] = matmul(tab_g[...].reshape(group, feats), ker[k], (1, 0)).astype(BF16).reshape(
-            8, rows, half)
+        hf, at = k // per_half, slice((k % per_half) * wide, (k % per_half + 1) * wide)
+        dxp[hf, :, :, at] = matmul(tab_g[...].reshape(group, feats), ker[k], (1, 0)).astype(
+            BF16).reshape(8, rows, wide)
         for j, (dy, dc) in enumerate(yc):
-            post(dxp.at[k, ((y + dy) % 4) * 2 + (c + dc) % 2], dx.at[k, me_g],
+            post(dxp.at[hf, ((y + dy) % 4) * 2 + (c + dc) % 2, :, at], dx.at[hf, me_g, :, at],
                  slot("dx_a2a", k * 8 + j), yc_peer(dy, dc), slot("dx_a2a") + k * 8 + me_g)
-        dx[k, me_g] = dxp[k, me_p]
+        dx[hf, me_g, :, at] = dxp[hf, me_p, :, at]
+    loss_row = column(fold(loss_part))
+    value = jnp.concatenate(
+        [fold(tab_back[:1]), fold(tab_back[1:]), loss_row, jnp.zeros((3, LANES), F32)], axis=0)
+    mine = bt_a.at[me_p]
+    mine[...] = value
+    bt_a_copies = [post(mine, mine, slot("bt_a", j), yc_peer(*to)) for j, to in enumerate(yc)]
+    bx_l[l] = jnp.concatenate([fold(t[i]) for i in (0, 1) for t in txt_back], axis=0)
+    bx_l_copy = post(bx_l.at[l], bx_l.at[l], slot("bx_l"), l_peer)
 
     def dx_wait(k, g):
         @pl.when(g != me_g)
         def _():
-            remote(dx.at[k, g], dx.at[k, g], slot("dx_a2a"), z_peer, slot("dx_a2a") + k * 8 + g).wait_recv()
+            for q in range(per_half):
+                ref = dx.at[k, g, :, q * wide:(q + 1) * wide]
+                remote(ref, ref, slot("dx_a2a"), z_peer,
+                       slot("dx_a2a") + (k * per_half + q) * 8 + g).wait_recv()
 
     txts = txt_g[...].reshape(group, feats)
-    both = (
-        matmul(txts[:, chunks[0]], ker[0], (1, 1)) + matmul(txts[:, chunks[1]], ker[1], (1, 1))
-    ).reshape(4, 2, rows, feats)
+    both = matmul(txts, jnp.concatenate([ker[k] for k in range(CHUNKS)], axis=1), (1, 1)).reshape(
+        4, 2, rows, feats)
     for k in (0, 1):
         dtp[k] = both[:, k]
     dt_c = post(dtp.at[1 - c], dt_cr, slot("dt_c"), c_peer)
@@ -439,6 +485,14 @@
     for k in (0, 1):
         if k == 1:
             dt_start()
+            for copy in bt_a_copies:
+                copy.wait_recv()
+            bt_b[zl] = jnp.sum(bt_a[...], axis=0)
+            bt_b_copies = [
+                post(bt_b.at[zl], bt_b.at[zl], slot("bt_b", i - 1), zl_peer(i)) for i in (1, 2, 3)]
+            bx_l_copy.wait_recv()
+            bx_x[x] = bx_l[0] + bx_l[1]
+            bx_x_copies = [post(bx_x.at[x], bx_x.at[x], slot("bx_x", i - 1), x_peer(i)) for i in (1, 2, 3)]
         for r, zz in zip(dxr, (zf, zh)):
             dx_wait(k, feat(zz, 2))
             r.send_opposite(k)
@@ -448,6 +502,10 @@
             dx_wait(k, feat(zz, (1, 3)[k]))
             r.pass_on(k)
             dx_wait(k, feat(zz, 0))
+    for copy in bx_x_copies:
+        copy.wait_recv()
+    bx_z[zh] = jnp.sum(bx_x[...], axis=0)
+    bx_z_copy = post(bx_z.at[zh], bx_z.at[zh], slot("bx_z"), z_peer)
     dt.pass_on(0)
     dt.pass_on(1)
     dx_z = []
@@ -457,26 +515,18 @@
     for k in (0, 1):
         d[TABLE, pl.ds(k * low, low)] = dt.total(k)
 
-    def backward_stats(side, extra=None):
-        v = d[side]
-        parts = [fold(column(v)), fold(column(v * z[side]))]
-        if extra is not None:
-            parts += [fold(extra), jnp.zeros((lanes, LANES), F32)]
-        stat_a(2 + side, jnp.concatenate(parts, axis=0))
-
-    def backward(side, inv):
-        total = stat_c(2 + side)
-        mean = unfold(total[:lanes]) / pairs
-        tilt = unfold(total[lanes:2 * lanes]) / pairs
-        return (inv * (d[side] - mean - z[side] * tilt)).astype(BF16), total
-
-    backward_stats(TABLE, loss_part)
-    for k, cols in enumerate(chunks):
-        v = dxr[NEAR].total(k)
-        dx_z[k].wait_recv()
-        d[TEXT, :, cols] = v + dx_zr[k].astype(F32)
-    stat_b(2 + TABLE)
-    backward_stats(TEXT)
+    for copy in bt_b_copies:
+        copy.wait_recv()
+    pair = [bt_b[h * 2], bt_b[h * 2 + 1]]
+    tilt_table, mean_table = [
+        jnp.concatenate([unfold(v[i:i + 2]) for v in pair], axis=1) for i in (0, 2)]
+
+    def backward(side, inv, mean, tilt):
+        return (inv * (d[side] - mean - z[side] * tilt)).astype(BF16)
+
+    loss_rows = jnp.sum(bt_b[...], axis=0)[4:5]
+    ls_x[x] = jnp.broadcast_to(jnp.sum(loss_rows, axis=1, keepdims=True), (8, LANES))
+    ls_copies = [post(ls_x.at[x], ls_x.at[x], slot("loss_x", i - 1), x_peer(i)) for i in (1, 2, 3)]
 
     def grad_reduce(side, where):
         def src(k, part_):
@@ -514,15 +564,22 @@
         gr[side][where].pass_on(0)
         gr[side][where].pass_on(1)
 
-    back_table, total = backward(TABLE, inv_table)
+    back_table = backward(TABLE, inv_table, mean_table, tilt_table)
     grad_terms(TABLE, FAR, back_table, gr[TABLE][FAR])
-    stat_b(2 + TEXT)
+    bx_z_copy.wait_recv()
+    bx_y[me_p] = bx_z[0] + bx_z[1]
+    bx_y_copies = [post(bx_y.at[me_p], bx_y.at[me_p], slot("bx_y", j), yc_peer(*to)) for j, to in enumerate(yc)]
     grad_terms(TABLE, NEAR, back_table, gr[TABLE][NEAR])
-    ls_x[0] = jnp.broadcast_to(
-        column(jnp.sum(total[2 * lanes:3 * lanes], axis=1, keepdims=True)), (8, LANES))
-    ls_copies = [post(ls_x.at[0], ls_x.at[i], slot("loss_x", i - 1), x_peer(i)) for i in (1, 2, 3)]
+    for k, cols in enumerate(halved):
+        v = dxr[NEAR].total(k)
+        dx_z[k].wait_recv()
+        d[TEXT, :, cols] = v + dx_zr[k].astype(F32)
     grad_pass(TABLE, FAR)
-    back_text, _ = backward(TEXT, inv_text)
+    for copy in bx_y_copies:
+        copy.wait_recv()
+    total = bx_y[(ft % 4) * 2 + ft // 4]
+    tilt_text, mean_text = unfold(total[:lanes]), unfold(total[lanes:])
+    back_text = backward(TEXT, inv_text, mean_text, tilt_text)
     grad_terms(TEXT, FAR, back_text, gr[TEXT][FAR])
     grad_far(TABLE)
     grad_pass(TABLE, NEAR)
@@ -530,8 +587,8 @@
     grad_pass(TEXT, FAR)
     for copy in ls_copies:
         copy.wait_recv()
-    ls_z[0] = jnp.sum(ls_x[...], axis=0)
-    ls_copy = post(ls_z.at[0], ls_z.at[1], slot("loss_z"), z_peer)
+    ls_z[zh] = jnp.sum(ls_x[...], axis=0)
+    ls_copy = post(ls_z.at[zh], ls_z.at[zh], slot("loss_z"), z_peer)
     grad_far(TEXT)
     grad_pass(TEXT, NEAR)
 
@@ -548,6 +605,21 @@
     grad_near(TEXT, grad_text)
     for wait in drain:
         wait()
+
+
+def hand_kernel(a, b, oa, ob):
+    oa[...] = a[...]
+    ob[...] = b[...]
+
+
+def hand_over(a, b):
+    vmem = pl.BlockSpec(memory_space=pltpu.VMEM)
+    return pl.pallas_call(
+        hand_kernel,
+        out_shape=(jax.ShapeDtypeStruct(a.shape, a.dtype), jax.ShapeDtypeStruct(b.shape, b.dtype)),
+        in_specs=[vmem, vmem], out_specs=(vmem, vmem),
+        name="hand_over",
+    )(a, b)
 
 
 def body(table, text, table_proj, text_proj):
@@ -570,13 +642,13 @@
             v((depth, feats), BF16), v((depth, feats), BF16),
             v((NUM_FEAT, 2, width, rows), BF16),
             v((2, rows, feats), F32),
-            v((4, 8, 16, LANES), F32), v((4, 4, 16, LANES), F32),
+            v((2, 8, 8, LANES), F32), v((2, 4, 8, LANES), F32),
             v((NUM_FEAT, rows, feats), BF16),
             v((8, rows, feats), BF16), v((8, rows, feats), BF16),
-            v((2, feats, half), F32),
-            v((2, half, half), BF16), v((2, half, half), BF16),
-            v((2, half, half), BF16), v((2, half, half), BF16),
-            v((2, feats, half), BF16),
+            v((feats, feats), F32),
+            v((CHUNKS, half, feats // CHUNKS), BF16), v((CHUNKS, half, feats // CHUNKS), BF16),
+            v((CHUNKS, half, feats // CHUNKS), BF16), v((CHUNKS, half, feats // CHUNKS), BF16),
+            v((CHUNKS, feats, feats // CHUNKS), BF16),
             v((2, 8, rows, half), BF16), v((2, 8, rows, half), BF16),
             v((2, 4, 2, rows, half), BF16),
             v((2, rows, half), BF16), v((2, rows, half), BF16),
@@ -587,6 +659,10 @@
             v((2, 2, 4, 2, width // 2, rows), BF16),
             v((2, width, rows), BF16), v((2, width, rows), BF16),
             v((4, 8, LANES), F32), v((2, 8, LANES), F32),
+            v((4, 8, LANES), F32),
+            v((8, 8, LANES), F32), v((4, 8, LANES), F32),
+            v((2, 8, LANES), F32), v((4, 8, LANES), F32),
+            v((2, 8, LANES), F32), v((8, 8, LANES), F32),
             pltpu.SemaphoreType.DMA((NUM_SLOTS,)),
             pltpu.SemaphoreType.DMA((NUM_SLOTS,)),
             pltpu.SemaphoreType.DMA((4,)),
@@ -597,6 +673,7 @@
         cost_estimate=pl.CostEstimate(flops=3_500_000_000, bytes_accessed=9_000_000, transcendentals=2048),
         name="barlow_step",
     )(table.T, text.T, table_proj, text_proj)
+    grad_table, grad_text = hand_over(grad_table, grad_text)
     return (grad_table.T, grad_text.T, loss.reshape(1))
 
 

time: 142 us -> 134 us (0.944); the launches traced: 140 us -> 134 us
  local copies, waits for them, and re-layouts: 3.28 us -> 0 us
  Pallas kernels: 134 us -> 132 us
    pallas_call x1, Pallas kernels: 134 us -> 130 us  [body(): pl.pallas_call(kernel, out_shape=(jax.ShapeDtypeStruct((width, rows), F32...]
    unnamed x2 -> x0, local copies, waits for them, and re-layouts: 3.28 us -> none
    pallas_call x0 -> x1, Pallas kernels: none -> 1.83 us  [hand_over(): pl.pallas_call(hand_kernel, out_shape=(jax.ShapeDtypeStruct(a.shape, a.dt...]
where the time goes in v3:
time: 134 us
  Pallas kernels  132 us (99%)
  between operations  2.4 us (2%)
    pallas_call x1, Pallas kernels, body(): pl.pallas_call(kernel, out_shape=(jax.ShapeDtypeStruct((width, rows), F32...  130 us

profile of v3, /device:TPU:32, one launch (start us, length us, event | category | flops | bytes accessed | tf_op | source)
XLA Modules:
  0.0 134.1 jit_solution(3280357236700192044)
XLA Ops:
  0.6 129.9 %barlow_step.1 = (f32[448,128]{1,0:T(8,128)}, f32[448,128]{1,0:T(8,128)}, f32[1,1]{1,0:T(1,128)}) custom-call(bf16[448,128]{1,0:T(8,128)(2,1)} %bitcast.7, bf16[448,128]{1,0:T(8,128)(2,1)} %bitcast.8, bf16[3584,512]{1,0:T(8,128)(2,1)} %tproj.1, bf16[3584,512]{1,0:T(8,128)(2,1)} %xproj.1), custom_call_target="tpu_custom_call" | custom-call | flops 3500000000 | bytes 9000000 | tf_op jit(solution)/shard_map/barlow_step/pallas_call | solution.py:632
  130.5 1.8 %hand_over.1 = (f32[448,128]{1,0:T(8,128)}, f32[448,128]{1,0:T(8,128)}) custom-call(f32[448,128]{1,0:T(8,128)} %get-tuple-element.8.a, f32[448,128]{1,0:T(8,128)} %get-tuple-element.9.b), custom_call_target="tpu_custom_call" | custom-call | tf_op jit(solution)/shard_map/hand_over/pallas_call | solution.py:617
